TPU v7x, 128 devices: a whole 4x4x4 slice. The times are simulated.
128 devices in a mesh: wide: 64 (over x, z, y_lo, core), narrow: 2 (over y_hi).
Axes of the slice: x: 4, y: 4 (y_hi: 2, y_lo: 2; y = y_hi * 2 + y_lo), z: 4, core: 2. Of those that a mesh axis runs over, the one named last changes fastest.
Arguments:
- dosage: bfloat16 [2048, 131072], P(None, 'wide'), may hold values from -4 to 6, as said below
- annotations: int32 [128, 131072], P(None, 'wide'), may hold values from 0 to 1, as said below
- test_statistic_table: float32 [131072, 512], P('wide', 'narrow'), may hold values from 0 to 200
Outputs:
- ld_scores: float32 [128, 131072], P(None, ('wide', 'narrow'))
- fitted: float32 [131072, 512], P('wide', 'narrow')
Inputs may be any that keep to these rules, and one draw needn't show every extreme that they name: `dosage`: dosages of each variant follow a correlated process along the variants. `annotations`: 1 where a variant belongs to an annotation.
All inputs are finite; a program needn't handle non-finite values.
Results may differ from a plain program's by a relative error of at most 0.0023.
Values may be sent and summed in bfloat16 or wider, within the bound.
A program may use at most 128 MiB of HBM per device.

v0:
```python
import jax
import jax.numpy as jnp
from jax import lax
from jax.sharding import PartitionSpec as P

HALF = 1024
highest_precision = lax.Precision.HIGHEST


def extended_2(cells, sides, width):
    for axis, dim in sides:
        count = lax.axis_size(axis)
        ends = count - 1
        head = lax.slice_in_dim(cells, 0, width, axis=dim)
        tail = lax.slice_in_dim(cells, cells.shape[dim] - width, cells.shape[dim], axis=dim)
        cells = jnp.concatenate(
            [
                lax.ppermute(tail, axis, [(i, (i + 1) % count) for i in range(ends)]),
                cells,
                lax.ppermute(head, axis, [((i + 1) % count, i) for i in range(ends)]),
            ],
            axis=dim,
        )
    return cells


def band_weights(col_geno, row_geno, col_start, row_start, total_variants):
    products = lax.dot_general(
        col_geno, row_geno, (((0,), (0,)), ((), ())), preferred_element_type=jnp.float32
    )
    samples = row_geno.shape[0]
    correlation = products / samples
    squared = correlation * correlation
    adjusted = squared - (1.0 - squared) / (samples - 2)
    col_index = col_start + jnp.arange(col_geno.shape[1], dtype=jnp.int32)[:, None]
    row_index = row_start + jnp.arange(row_geno.shape[1], dtype=jnp.int32)[None, :]
    inside = (
        (jnp.abs(row_index - col_index) <= HALF) & (col_index >= 0) & (col_index < total_variants)
    )
    return jnp.where(inside, adjusted, 0.0).astype(jnp.bfloat16)


def shards(dosage, annotations, test_statistic_table):
    samples = dosage.shape[0]
    strip_cols = dosage.shape[1]
    half_width = strip_cols // 2
    total_variants = lax.axis_size("wide") * strip_cols
    wide_index = lax.axis_index("wide")
    narrow_index = lax.axis_index("narrow")
    values = dosage.astype(jnp.float32)
    average = jnp.mean(values, axis=0)
    centred_values = values - average[None, :]
    variance = jnp.mean(centred_values * centred_values, axis=0)
    standard = (centred_values / jnp.sqrt(variance + 1e-05)[None, :]).astype(jnp.bfloat16)
    counts = lax.psum(jnp.sum(annotations.astype(jnp.float32), axis=1), "wide")
    shares = counts / total_variants
    centred = (annotations.astype(jnp.float32) - shares[:, None]).astype(jnp.bfloat16)
    stacked = jnp.concatenate([standard, centred], axis=0)
    row_local = narrow_index * half_width
    strip_start = wide_index * strip_cols
    row_start = strip_start + row_local
    own_rows = lax.dynamic_slice_in_dim(standard, row_local, half_width, 1)
    extended = extended_2(stacked, (("wide", 1),), half_width)
    scores = jnp.zeros((centred.shape[0], half_width), jnp.float32)
    for offset in range(3):
        col_block = lax.dynamic_slice_in_dim(
            extended, row_local + offset * half_width, half_width, 1
        )
        weights = band_weights(
            col_block[:samples],
            own_rows,
            row_start - half_width + offset * half_width,
            row_start,
            total_variants,
        )
        scores = scores + jnp.dot(col_block[samples:], weights, preferred_element_type=jnp.float32)
    strip_scores = lax.all_gather(scores, "narrow", axis=1, tiled=True)
    chi_local = jnp.sum(test_statistic_table, axis=0)
    totals = lax.psum(jnp.sum(strip_scores, axis=1), "wide")
    score_mean = totals / total_variants
    deviation = strip_scores - score_mean[:, None]
    cross_local = lax.dot_general(
        deviation,
        deviation,
        (((1,), (1,)), ((), ())),
        precision=highest_precision,
        preferred_element_type=jnp.float32,
    )
    proj_local = jnp.dot(
        deviation,
        test_statistic_table,
        precision=highest_precision,
        preferred_element_type=jnp.float32,
    )
    cross_sum, proj_sum, dev_sum, chi_sum = lax.psum(
        (cross_local, proj_local, jnp.sum(deviation, axis=1), chi_local), "wide"
    )
    chi_mean = chi_sum / total_variants
    covariance = cross_sum / total_variants
    centred_proj = (
        proj_sum / total_variants - (dev_sum / total_variants)[:, None] * chi_mean[None, :]
    )
    spread = jnp.sqrt(jnp.diagonal(covariance) + 1e-05)
    gram_matrix = covariance / (spread[:, None] * spread[None, :])
    projection = centred_proj / spread[:, None]
    factor = jnp.linalg.cholesky(gram_matrix)
    coefficient = jax.scipy.linalg.cho_solve((factor, True), projection)
    standard_scores = (strip_scores - score_mean[:, None]) / spread[:, None]
    fitted = chi_mean[None, :] + lax.dot_general(
        standard_scores,
        coefficient,
        (((0,), (0,)), ((), ())),
        precision=highest_precision,
        preferred_element_type=jnp.float32,
    )
    own_scores = lax.dynamic_slice_in_dim(standard_scores, row_local, half_width, 1)
    return (own_scores, fitted)


def solution(mesh):
    in_specs = (P(None, "wide"), P(None, "wide"), P("wide", "narrow"))
    out_specs = (P(None, ("wide", "narrow")), P("wide", "narrow"))
    return jax.shard_map(shards, mesh=mesh, in_specs=in_specs, out_specs=out_specs, check_vma=False)
```

profile of v0, /device:TPU:0, one launch (start us, length us, event | category | flops | bytes accessed | tf_op | source)
XLA Modules:
  0.0 1175.0 jit_solution(18052722490963843743)
XLA Ops:
  7.2 0.0 all-gather.2.cloned.1.call-start
  7.2 0.0 copy-start
  7.2 4.9 convert_reduce_fusion
  12.2 0.8 copy-done
  13.0 2.2 fusion.2
  15.2 0.0 copy-start.3
  15.2 10.0 fusion.3
  25.2 0.0 copy-done.3
  25.2 0.2 convert_reduce_fusion.1
  25.4 145.3 %psum.42 = f32[128]{0:T(128)S(1)} all-reduce(f32[128]{0:T(128)S(1)} %convert_reduce_fusion.1), channel_id=1, replica_groups=mesh['wide'=64,'narrow'=2] {'wide'}, use_global_device_ids=true, to_apply=%region_3.0 | all-reduce | flops 128 | bytes 1024 | tf_op jit(solution)/shard_map/psum | solution.py:55
  170.7 0.2 subtract_convert_fusion
  170.9 12.3 %fusion.4 = (bf16[2176,1024]{1,0:T(8,128)(2,1)}, bf16[2176,1024]{1,0:T(8,128)(2,1)}) fusion(bf16[2048,2048]{1,0:T(8,128)(2,1)} %fusion.3, bf16[128,2048]{1,0:T(8,128)(2,1)S(1)} %subtract_convert_fusion), kind=kLoop, calls=%fused_computation.10 | loop fusion | flops 17825792 | bytes 17825792 | tf_op jit(solution)/shard_map/concatenate | solution.py:58
  183.2 1.3 collective-permute-start.1
  184.5 5.2 collective-permute-start
  189.8 3.2 collective-permute-done.1
  193.0 2.1 collective-permute-done
  195.0 23.0 %pad_maximum_fusion = bf16[2176,4096]{1,0:T(8,128)(2,1)} fusion(bf16[2176,1024]{1,0:T(8,128)(2,1)} %collective-permute-done.1, bf16[128,2048]{1,0:T(8,128)(2,1)S(1)} %subtract_convert_fusion, bf16[2048,2048]{1,0:T(8,128)(2,1)} %fusion.3, bf16[2176,1024]{1,0:T(8,128)(2,1)} %collective-permute-done), kind=kLoop, calls=%fused_computation.5 | loop fusion | flops 71303168 | bytes 35651584 | tf_op jit(solution)/shard_map/concatenate | solution.py:16
  218.1 10.2 fusion.39
  228.2 11.2 fusion.44
  239.4 11.1 fusion.52
  250.5 0.0 all-gather.2.cloned.1.call-update
  250.5 0.0 all-reduce.4.cloned.1.call-start
  250.6 106.2 %all-gather.2.cloned.1.call-done = f32[128,2048]{1,0:T(8,128)} async-done(((f32[128,1024]{1,0:T(8,128)}), f32[128,2048]{1,0:T(8,128)}) %all-gather.2.cloned.1.call-update) | async-done | bytes 1048592 | tf_op jit(solution)/shard_map/all_gather | solution.py:77
  356.8 1.4 reduce_sum.57
  358.2 143.0 %psum.43 = f32[128]{0:T(128)S(1)} all-reduce(f32[128]{0:T(128)S(1)} %reduce_sum.57), channel_id=1, replica_groups=mesh['wide'=64,'narrow'=2] {'wide'}, use_global_device_ids=true, to_apply=%region_5.6 | all-reduce | flops 128 | bytes 1024 | tf_op jit(solution)/shard_map/psum | solution.py:79
  501.2 3.3 fusion.59
  504.5 0.0 copy-done.2
  504.5 3.1 fusion.57
  507.6 0.0 all-reduce.4.cloned.1.call-update
  507.6 0.3 reduce_sum.58
  507.9 488.1 %all-reduce.4.cloned.1.call-done = (f32[128,128]{0,1:T(8,128)}, f32[128,256]{1,0:T(8,128)}) async-done(((f32[128,128]{0,1:T(8,128)}, f32[128,256]{1,0:T(8,128)}), (f32[128,128]{0,1:T(8,128)}, f32[128,256]{1,0:T(8,128)})) %all-reduce.4.cloned.1.call-update) | async-done | bytes 196624 | tf_op jit(solution)/shard_map/psum | solution.py:95
  996.0 0.9 broadcast_multiply_fusion
  996.9 1.3 gather_fusion
  998.2 0.9 multiply_divide_fusion
  999.1 0.0 copy-done.1
  999.1 0.3 subtract_reduce_fusion
  999.4 0.8 constant_dynamic-slice_fusion
  1000.2 0.1 copy.8
  1000.3 0.9 fusion.75
  1001.3 11.7 cholesky.16
  1013.0 0.6 compare_reduce_fusion
  1013.7 0.7 fusion.71
  1014.3 9.8 custom-call.10
  1024.2 139.8 %all-reduce = (f32[256]{0:T(256)S(1)}, f32[128]{0:T(128)S(1)}) all-reduce(f32[256]{0:T(256)S(1)} %reduce_sum.58, f32[128]{0:T(128)S(1)} %get-tuple-element.8), channel_id=1, replica_groups=mesh['wide'=64,'narrow'=2] {'wide'}, use_global_device_ids=true, to_apply=%region_8.9 | all-reduce | flops 384 | bytes 3072 | tf_op jit(solution)/shard_map/psum | solution.py:95
  1164.0 0.0 copy-done.4
  1164.0 0.4 fusion.66
  1164.4 0.3 fusion.72
  1164.7 3.2 convolution_add_fusion
  (17 shorter events, 0.1 us)
Async XLA Ops:
  7.2 349.6 %all-gather.2.cloned.1.call-start = ((), (), s32[]{:S(2)}) async-start(), calls=%async_computation | async-start | bytes 1572864 | tf_op jit(solution)/shard_map/all_gather | solution.py:77
  7.2 5.8 copy-start
  15.2 10.0 copy-start.3
  183.2 9.8 collective-permute-start.1
  184.5 10.5 collective-permute-start
  239.4 265.1 %copy-start.2 = (f32[2048,256]{1,0:T(8,128)S(1)}, f32[2048,256]{1,0:T(8,128)}, u32[]{:S(2)}) copy-start(f32[2048,256]{1,0:T(8,128)} %param.5) | copy-start | bytes 6291460
  250.5 745.5 %all-reduce.4.cloned.1.call-start = ((), (), s32[]{:S(2)}) async-start(), calls=%async_computation.1 | async-start | bytes 393216 | tf_op jit(solution)/shard_map/psum | solution.py:95
  356.8 642.4 %copy-start.1 = (f32[128,2048]{1,0:T(8,128)S(1)}, f32[128,2048]{1,0:T(8,128)}, u32[]{:S(2)}) copy-start(f32[128,2048]{1,0:T(8,128)} %all-gather.2.cloned.1.call-done) | copy-start | bytes 3145732
  996.0 168.0 %copy-start.4 = (f32[128,256]{1,0:T(8,128)S(1)}, f32[128,256]{1,0:T(8,128)}, u32[]{:S(2)}) copy-start(f32[128,256]{1,0:T(8,128)} %get-tuple-element.5) | copy-start | bytes 393220
Sparse Core Ops, SparseCore 0:
  250.7 106.0 all-gather.1
  507.7 488.2 all-reduce.3
where the time goes:
time: 1180 us
  waiting for transfers between devices  600 us (51%)
  blocking collectives  428 us (36%)
  other arithmetic  80.5 us (7%)
  matrix products  42.6 us (4%)
  between operations  14.6 us (1%)
    psum x1, waiting for transfers between devices, shards(): lax.psum((cross_local, proj_local, jnp.sum(deviation, axis=1), chi_local)...  488 us
    psum x1, blocking collectives, shards(): counts = lax.psum(jnp.sum(annotations.astype(jnp.float32), axis=1), 'wide')  145 us
    psum x1, blocking collectives, shards(): totals = lax.psum(jnp.sum(strip_scores, axis=1), 'wide')  143 us
    psum x1, blocking collectives, shards(): lax.psum((cross_local, proj_local, jnp.sum(deviation, axis=1), chi_local)...  140 us
    all_gather x1, waiting for transfers between devices, shards(): strip_scores = lax.all_gather(scores, 'narrow', axis=1, tiled=True)  106 us
    dot_general x3, matrix products, shards(): jnp.dot(col_block[samples:], weights, preferred_element_type=jnp.float32)  32.5 us
  transfers between devices with their start and end apart: 4, of which 4 were waited for; matrix products, arithmetic and copies ran while one was open for 0% of the time, Pallas kernels for 0%

commit v1 on v0

--- a/solution.py
+++ b/solution.py
@@ -76,7 +76,7 @@
         scores = scores + jnp.dot(col_block[samples:], weights, preferred_element_type=jnp.float32)
     strip_scores = lax.all_gather(scores, "narrow", axis=1, tiled=True)
     chi_local = jnp.sum(test_statistic_table, axis=0)
-    totals = lax.psum(jnp.sum(strip_scores, axis=1), "wide")
+    totals = jnp.sum(lax.all_gather(jnp.sum(strip_scores, axis=1), "wide"), axis=0)
     score_mean = totals / total_variants
     deviation = strip_scores - score_mean[:, None]
     cross_local = lax.dot_general(

time: 1180 us -> 1120 us (0.949)
  blocking collectives: 428 us -> 366 us
    psum x1 -> x0, blocking collectives: 143 us -> none  [shards(): totals = lax.psum(jnp.sum(strip_scores, axis=1), 'wide')]
    all_gather x0 -> x1, blocking collectives: none -> 80.8 us  [shards(): lax.all_gather(jnp.sum(strip_scores, axis=1), 'wide')]
where the time goes in v1:
time: 1120 us; the launch traced here: 1110 us
  waiting for transfers between devices  599 us (53%)
  blocking collectives  366 us (33%)
  other arithmetic  80.6 us (7%)
  matrix products  41.6 us (4%)
  between operations  14.5 us (1%)
    psum x1, waiting for transfers between devices, shards(): lax.psum((cross_local, proj_local, jnp.sum(deviation, axis=1), chi_local)...  488 us
    psum x1, blocking collectives, shards(): counts = lax.psum(jnp.sum(annotations.astype(jnp.float32), axis=1), 'wide')  145 us
    psum x1, blocking collectives, shards(): lax.psum((cross_local, proj_local, jnp.sum(deviation, axis=1), chi_local)...  140 us
    all_gather x1, waiting for transfers between devices, shards(): strip_scores = lax.all_gather(scores, 'narrow', axis=1, tiled=True)  106 us
    all_gather x1, blocking collectives, shards(): lax.all_gather(jnp.sum(strip_scores, axis=1), 'wide')  80.8 us
    dot_general x3, matrix products, shards(): jnp.dot(col_block[samples:], weights, preferred_element_type=jnp.float32)  31.5 us
    concatenate x1, other arithmetic, extended_2(): jnp.concatenate([lax.ppermute(tail, axis, [(i, (i + 1) % count) for i in...  23 us
  transfers between devices with their start and end apart: 4, of which 4 were waited for; matrix products, arithmetic and copies ran while one was open for 0% of the time, Pallas kernels for 0%

profile of v1, /device:TPU:0, one launch (start us, length us, event | category | flops | bytes accessed | tf_op | source)
XLA Modules:
  0.0 1112.0 jit_solution(12936272461051831807)
XLA Ops:
  7.2 0.0 all-gather.4.cloned.1.call-start
  7.2 0.0 copy-start
  7.2 4.9 convert_reduce_fusion
  12.2 0.8 copy-done
  13.0 2.2 fusion.2
  15.2 10.0 fusion.3
  25.2 0.0 copy-done.3
  25.2 0.2 convert_reduce_fusion.1
  25.4 145.3 %psum.35 = f32[128]{0:T(128)S(1)} all-reduce(f32[128]{0:T(128)S(1)} %convert_reduce_fusion.1), channel_id=1, replica_groups=mesh['wide'=64,'narrow'=2] {'wide'}, use_global_device_ids=true, to_apply=%region_3.0 | all-reduce | flops 128 | bytes 1024 | tf_op jit(solution)/shard_map/psum | solution.py:55
  170.7 0.2 subtract_convert_fusion
  170.9 12.3 %fusion.4 = (bf16[2176,1024]{1,0:T(8,128)(2,1)}, bf16[2176,1024]{1,0:T(8,128)(2,1)}) fusion(bf16[2048,2048]{1,0:T(8,128)(2,1)} %fusion.3, bf16[128,2048]{1,0:T(8,128)(2,1)S(1)} %subtract_convert_fusion), kind=kLoop, calls=%fused_computation.10 | loop fusion | flops 17825792 | bytes 17825792 | tf_op jit(solution)/shard_map/concatenate | solution.py:58
  183.2 1.3 collective-permute-start.1
  184.5 5.5 collective-permute-start
  190.1 2.9 collective-permute-done.1
  193.0 2.1 collective-permute-done
  195.0 23.0 %pad_maximum_fusion = bf16[2176,4096]{1,0:T(8,128)(2,1)} fusion(bf16[2176,1024]{1,0:T(8,128)(2,1)} %collective-permute-done.1, bf16[128,2048]{1,0:T(8,128)(2,1)S(1)} %subtract_convert_fusion, bf16[2048,2048]{1,0:T(8,128)(2,1)} %fusion.3, bf16[2176,1024]{1,0:T(8,128)(2,1)} %collective-permute-done), kind=kLoop, calls=%fused_computation.5 | loop fusion | flops 71303168 | bytes 35651584 | tf_op jit(solution)/shard_map/concatenate | solution.py:16
  218.1 10.1 fusion.39
  228.2 10.3 fusion.44
  238.5 11.0 fusion.52
  249.5 0.0 all-gather.4.cloned.1.call-update
  249.6 0.0 all-reduce.4.cloned.1.call-start
  249.6 106.2 %all-gather.4.cloned.1.call-done = f32[128,2048]{1,0:T(8,128)} async-done(((f32[128,1024]{1,0:T(8,128)}), f32[128,2048]{1,0:T(8,128)}) %all-gather.4.cloned.1.call-update) | async-done | bytes 1048592 | tf_op jit(solution)/shard_map/all_gather | solution.py:77
  355.8 1.4 reduce_sum.66
  357.2 80.8 %all-gather.1 = f32[64,1,128]{2,1,0:T(1,128)S(1)} all-gather(f32[1,1,128]{2,1,0:T(1,128)S(1)} %bitcast.18), channel_id=2, replica_groups=mesh['wide'=64,'narrow'=2] {'wide'}, dimensions={0}, use_global_device_ids=true | all-gather | bytes 33280 | tf_op jit(solution)/shard_map/all_gather | solution.py:79
  438.1 0.1 reduce_sum.67
  438.1 3.3 fusion.59
  441.5 0.0 copy-done.2
  441.5 3.1 fusion.57
  444.5 0.0 all-reduce.4.cloned.1.call-update
  444.6 0.3 reduce_sum.68
  444.9 488.1 %all-reduce.4.cloned.1.call-done = (f32[128,128]{0,1:T(8,128)}, f32[128,256]{1,0:T(8,128)}) async-done(((f32[128,128]{0,1:T(8,128)}, f32[128,256]{1,0:T(8,128)}), (f32[128,128]{0,1:T(8,128)}, f32[128,256]{1,0:T(8,128)})) %all-reduce.4.cloned.1.call-update) | async-done | bytes 196624 | tf_op jit(solution)/shard_map/psum | solution.py:95
  933.0 0.9 broadcast_multiply_fusion
  933.8 1.5 gather_fusion
  935.3 0.9 multiply_divide_fusion
  936.3 0.0 copy-done.1
  936.3 0.3 subtract_reduce_fusion
  936.6 0.8 constant_dynamic-slice_fusion
  937.4 0.1 copy.10
  937.5 0.9 fusion.75
  938.4 11.7 %cholesky.16 = f32[128,128]{1,0:T(8,128)S(1)} custom-call(f32[128,128]{1,0:T(8,128)S(1)} %fusion.75), custom_call_target="Cholesky" | custom-call | tf_op jit(solution)/shard_map/jit(cholesky)/cholesky | solution.py:106
  950.2 0.6 compare_reduce_fusion
  950.8 0.7 fusion.71
  951.5 9.8 custom-call.10
  961.3 139.8 %all-reduce = (f32[256]{0:T(256)S(1)}, f32[128]{0:T(128)S(1)}) all-reduce(f32[256]{0:T(256)S(1)} %reduce_sum.68, f32[128]{0:T(128)S(1)} %get-tuple-element.8), channel_id=1, replica_groups=mesh['wide'=64,'narrow'=2] {'wide'}, use_global_device_ids=true, to_apply=%region_8.9 | all-reduce | flops 384 | bytes 3072 | tf_op jit(solution)/shard_map/psum | solution.py:95
  1101.2 0.0 copy-done.4
  1101.2 0.4 fusion.66
  1101.5 0.3 fusion.72
  1101.8 3.2 convolution_add_fusion
  (18 shorter events, 0.1 us)
Async XLA Ops:
  7.2 348.6 %all-gather.4.cloned.1.call-start = ((), (), s32[]{:S(2)}) async-start(), calls=%async_computation | async-start | bytes 1572864 | tf_op jit(solution)/shard_map/all_gather | solution.py:77
  7.2 5.8 copy-start
  15.2 10.0 copy-start.3
  183.2 9.8 collective-permute-start.1
  184.5 10.5 collective-permute-start
  249.5 191.9 %copy-start.2 = (f32[2048,256]{1,0:T(8,128)S(1)}, f32[2048,256]{1,0:T(8,128)}, u32[]{:S(2)}) copy-start(f32[2048,256]{1,0:T(8,128)} %param.5) | copy-start | bytes 6291460
  249.6 683.4 %all-reduce.4.cloned.1.call-start = ((), (), s32[]{:S(2)}) async-start(), calls=%async_computation.1 | async-start | bytes 393216 | tf_op jit(solution)/shard_map/psum | solution.py:95
  355.8 580.5 %copy-start.1 = (f32[128,2048]{1,0:T(8,128)S(1)}, f32[128,2048]{1,0:T(8,128)}, u32[]{:S(2)}) copy-start(f32[128,2048]{1,0:T(8,128)} %all-gather.4.cloned.1.call-done) | copy-start | bytes 3145732
  933.0 168.2 %copy-start.4 = (f32[128,256]{1,0:T(8,128)S(1)}, f32[128,256]{1,0:T(8,128)}, u32[]{:S(2)}) copy-start(f32[128,256]{1,0:T(8,128)} %get-tuple-element.5) | copy-start | bytes 393220
Sparse Core Ops, SparseCore 0:
  249.7 106.0 all-gather.3
  444.7 488.2 all-reduce.3

commit v2 on v0

--- a/solution.py
+++ b/solution.py
@@ -74,7 +74,9 @@
             total_variants,
         )
         scores = scores + jnp.dot(col_block[samples:], weights, preferred_element_type=jnp.float32)
-    strip_scores = lax.all_gather(scores, "narrow", axis=1, tiled=True)
+    strip_scores = jnp.concatenate(
+        lax.all_to_all(jnp.stack([scores] * lax.axis_size("narrow")), "narrow", 0, 0), axis=1
+    )
     chi_local = jnp.sum(test_statistic_table, axis=0)
     totals = lax.psum(jnp.sum(strip_scores, axis=1), "wide")
     score_mean = totals / total_variants

time: 1180 us -> 1160 us (0.983)
  waiting for transfers between devices: 600 us -> 507 us
  blocking collectives: 428 us -> 499 us
    all_gather x1 -> x0, waiting for transfers between devices: 106 us -> none  [shards(): strip_scores = lax.all_gather(scores, 'narrow', axis=1, tiled=True)]
    psum x1, blocking collectives: 143 us -> 215 us  [shards(): totals = lax.psum(jnp.sum(strip_scores, axis=1), 'wide')]
    all_to_all x0 -> x1, waiting for transfers between devices: none -> 14.2 us  [shards(): lax.all_to_all(jnp.stack([scores] * lax.axis_size('narrow')), 'narrow', 0...]
where the time goes in v2:
time: 1160 us
  waiting for transfers between devices  507 us (44%)
  blocking collectives  499 us (43%)
  other arithmetic  81.2 us (7%)
  matrix products  40.4 us (3%)
  between operations  14.5 us (1%)
    psum x1, waiting for transfers between devices, shards(): lax.psum((cross_local, proj_local, jnp.sum(deviation, axis=1), chi_local)...  488 us
    psum x1, blocking collectives, shards(): totals = lax.psum(jnp.sum(strip_scores, axis=1), 'wide')  215 us
    psum x1, blocking collectives, shards(): counts = lax.psum(jnp.sum(annotations.astype(jnp.float32), axis=1), 'wide')  145 us
    psum x1, blocking collectives, shards(): lax.psum((cross_local, proj_local, jnp.sum(deviation, axis=1), chi_local)...  139 us
    dot_general x3, matrix products, shards(): jnp.dot(col_block[samples:], weights, preferred_element_type=jnp.float32)  30.7 us
  transfers between devices with their start and end apart: 4, of which 4 were waited for; matrix products, arithmetic and copies ran while one was open for 0% of the time, Pallas kernels for 0%

profile of v2, /device:TPU:0, one launch (start us, length us, event | category | flops | bytes accessed | tf_op | source)
XLA Modules:
  0.0 1155.9 jit_solution(7762758721864435997)
XLA Ops:
  7.2 0.0 copy-start
  7.2 4.9 convert_reduce_fusion
  12.1 0.8 copy-done
  12.9 2.2 fusion.2
  15.2 10.0 fusion.3
  25.2 0.0 copy-done.1
  25.2 0.2 convert_reduce_fusion.1
  25.4 145.3 %psum.42 = f32[128]{0:T(128)S(1)} all-reduce(f32[128]{0:T(128)S(1)} %convert_reduce_fusion.1), channel_id=1, replica_groups=mesh['wide'=64,'narrow'=2] {'wide'}, use_global_device_ids=true, to_apply=%region_3.0 | all-reduce | flops 128 | bytes 1024 | tf_op jit(solution)/shard_map/psum | solution.py:55
  170.7 0.2 subtract_convert_fusion
  170.8 12.3 %fusion.4 = (bf16[2176,1024]{1,0:T(8,128)(2,1)}, bf16[2176,1024]{1,0:T(8,128)(2,1)}) fusion(bf16[2048,2048]{1,0:T(8,128)(2,1)} %fusion.3, bf16[128,2048]{1,0:T(8,128)(2,1)S(1)} %subtract_convert_fusion), kind=kLoop, calls=%fused_computation.10 | loop fusion | flops 17825792 | bytes 17825792 | tf_op jit(solution)/shard_map/concatenate | solution.py:58
  183.2 1.3 collective-permute-start.1
  184.5 5.5 collective-permute-start
  190.0 2.9 collective-permute-done.1
  192.9 2.1 collective-permute-done
  195.0 23.0 %pad_maximum_fusion = bf16[2176,4096]{1,0:T(8,128)(2,1)} fusion(bf16[2176,1024]{1,0:T(8,128)(2,1)} %collective-permute-done.1, bf16[128,2048]{1,0:T(8,128)(2,1)S(1)} %subtract_convert_fusion, bf16[2048,2048]{1,0:T(8,128)(2,1)} %fusion.3, bf16[2176,1024]{1,0:T(8,128)(2,1)} %collective-permute-done), kind=kLoop, calls=%fused_computation.5 | loop fusion | flops 71303168 | bytes 35651584 | tf_op jit(solution)/shard_map/concatenate | solution.py:16
  218.0 10.1 fusion.39
  228.2 10.3 fusion.44
  238.5 10.2 fusion.57
  248.7 1.1 pad_maximum_fusion.2
  249.8 4.2 all-to-all-start
  254.0 0.0 all-reduce.4.cloned.1.call-start
  254.0 1.9 reduce_sum.58
  255.8 14.2 %all-to-all-done = f32[2,128,1024]{2,1,0:T(8,128)S(1)} async-done(((f32[2,128,1024]{2,1,0:T(8,128)}), f32[2,128,1024]{2,1,0:T(8,128)S(1)}, u32[]{:S(2)}, u32[]{:S(2)}) %all-to-all-start) | async-done | bytes 1048608 | tf_op jit(solution)/shard_map/all_to_all | solution.py:78
  270.1 0.1 reduce_sum.57
  270.2 214.7 %psum.43 = f32[128]{0:T(128)S(1)} all-reduce(f32[128]{0:T(128)S(1)} %reduce_sum.57), channel_id=1, replica_groups=mesh['wide'=64,'narrow'=2] {'wide'}, use_global_device_ids=true, to_apply=%region_5.6 | all-reduce | flops 128 | bytes 1024 | tf_op jit(solution)/shard_map/psum | solution.py:81
  484.9 0.3 copy.7
  485.2 0.1 bitcast_subtract_fusion
  485.3 4.2 fusion.110
  489.5 0.2 subtract_reduce_fusion
  489.7 138.6 %all-reduce = (f32[256]{0:T(256)S(1)}, f32[128]{0:T(128)S(1)}) all-reduce(f32[256]{0:T(256)S(1)} %reduce_sum.58, f32[128]{0:T(128)S(1)} %subtract_reduce_fusion), channel_id=1, replica_groups=mesh['wide'=64,'narrow'=2] {'wide'}, use_global_device_ids=true, to_apply=%region_8.9 | all-reduce | flops 384 | bytes 3072 | tf_op jit(solution)/shard_map/psum | solution.py:97
  628.4 1.8 convolution_bitcast_fusion
  630.1 0.0 all-reduce.4.cloned.1.call-update
  630.2 487.5 %all-reduce.4.cloned.1.call-done = (f32[128,128]{0,1:T(8,128)}, f32[128,256]{1,0:T(8,128)}) async-done(((f32[128,128]{0,1:T(8,128)}, f32[128,256]{1,0:T(8,128)}), (f32[128,128]{0,1:T(8,128)}, f32[128,256]{1,0:T(8,128)})) %all-reduce.4.cloned.1.call-update) | async-done | bytes 196624 | tf_op jit(solution)/shard_map/psum | solution.py:97
  1117.7 0.9 broadcast_multiply_fusion
  1118.6 1.3 gather_fusion
  1119.9 0.1 broadcast_divide_fusion
  1120.0 0.9 multiply_divide_fusion
  1121.0 1.0 copy.10
  1122.0 0.1 copy.9
  1122.1 0.0 copy-done.2
  1122.1 0.1 fusion.76
  1122.2 11.7 %cholesky.16 = f32[128,128]{1,0:T(8,128)S(1)} custom-call(f32[128,128]{1,0:T(8,128)S(1)} %fusion.76), custom_call_target="Cholesky" | custom-call | tf_op jit(solution)/shard_map/jit(cholesky)/cholesky | solution.py:108
  1133.9 0.6 compare_reduce_fusion
  1134.6 0.7 fusion.72
  1135.2 9.8 custom-call.10
  1145.1 0.4 fusion.67
  1145.4 0.3 fusion.73
  1145.7 3.1 convolution_add_fusion
  (19 shorter events, 0.2 us)
Async XLA Ops:
  7.2 5.8 copy-start
  15.2 10.0 copy-start.1
  183.2 9.8 collective-permute-start.1
  184.5 10.5 collective-permute-start
  249.8 20.3 %all-to-all-start = ((f32[2,128,1024]{2,1,0:T(8,128)}), f32[2,128,1024]{2,1,0:T(8,128)S(1)}, u32[]{:S(2)}, u32[]{:S(2)}) async-start(f32[2,128,1024]{2,1,0:T(8,128)} %pad_maximum_fusion.2), calls=%async_computation | async-start | bytes 2097152 | tf_op jit(solution)/shard_map/all_to_all | solution.py:78
  254.0 863.7 %all-reduce.4.cloned.1.call-start = ((), (), s32[]{:S(2)}) async-start(), calls=%async_computation.1 | async-start | bytes 393216 | tf_op jit(solution)/shard_map/psum | solution.py:97
  1117.7 4.4 copy-start.2
  1117.7 27.4 %copy-start.3 = (f32[128,256]{1,0:T(8,128)S(1)}, f32[128,256]{1,0:T(8,128)}, u32[]{:S(2)}) copy-start(f32[128,256]{1,0:T(8,128)} %get-tuple-element.7) | copy-start | bytes 393220
Sparse Core Ops, SparseCore 0:
  630.3 487.3 all-reduce.3
